TPU v7x, 512 devices: a whole 4x8x8 slice. The times are simulated.
512 devices in a mesh: fft: 32 (over y, x_hi, core), plane: 16 (over z, x_lo).
Axes of the slice: x: 4 (x_hi: 2, x_lo: 2; x = x_hi * 2 + x_lo), y: 8, z: 8, core: 2. Of those that a mesh axis runs over, the one named last changes fastest.
Arguments:
- error_field: float32 [2048, 16, 2048], P('fft', 'plane'), may hold values from -1 to 1
- x_shape: float32 [2048], replicated, may hold values from 0.25 to 1
- y_shape: float32 [2048], replicated, may hold values from 0.25 to 1
Outputs:
- corrected: float32 [2048, 16, 2048], P('fft', 'plane')
All inputs are finite; a program needn't handle non-finite values.
Results may differ from a plain program's by a relative error of at most 0.00012.
Values sent between devices are 32-bit elements; how exact they have to be, the bound alone decides.
A program may use at most 64 MiB of HBM per device.

v0:
```python
import math

import jax
import jax.numpy as jnp
import ml_dtypes
import numpy as np
from jax import lax
from jax.experimental import pallas as pl
from jax.experimental.pallas import tpu as pltpu
from jax.sharding import PartitionSpec as P

F32 = jnp.float32
BF16 = jnp.bfloat16
N = 2048
FFT = 32
PLANES = 16
OWN = N // FFT
HALF = 64
LANES = 128
CHUNKS = 2
MESH = pl.DeviceIdType.MESH


def two_parts(table):
    table = np.asarray(table, np.float64)
    high = table.astype(np.float32).astype(ml_dtypes.bfloat16)
    low = (table - high.astype(np.float64)).astype(np.float32).astype(ml_dtypes.bfloat16)
    return np.stack([high, low])


def row_order():
    chunk, block, part, step = np.meshgrid(np.arange(2), np.arange(4), np.arange(2), np.arange(8), indexing="ij")
    return part.reshape(-1), (block * 16 + chunk * 8 + step).reshape(-1)


def y_forward_table():
    part, row = row_order()
    angle = 2 * np.pi / LANES * (row[:, None] * np.arange(LANES)[None, :] % LANES)
    cosine, sine = np.cos(angle), np.sin(angle)
    part = part[:, None]
    table = np.concatenate([np.where(part == 0, cosine, -sine), np.where(part == 0, sine, cosine)], 1)
    extra = np.zeros((16, 2 * LANES))
    extra[0, :LANES] = 1 - 2 * (np.arange(LANES) % 2)
    return two_parts(np.concatenate([table, extra], 0))


def y_inverse_table():
    part, row = row_order()
    column = np.arange(LANES)
    angle = 2 * np.pi / LANES * (row[:, None] * column[None, :] % LANES)
    cosine, sine = np.cos(angle), np.sin(angle)
    part, row = part[:, None], row[:, None]
    plain = np.concatenate([np.where(part == 0, cosine, -sine), np.where(part == 0, sine, cosine)], 1)
    sign = (1 - 2 * (column % 2))[None, :]
    first = np.where(part == 0, np.where(row == 0, 1.0, 2 * cosine), np.where(row == 0, sign, -2 * sine))
    return two_parts(np.concatenate([plain, first], 1) / (N * N))


def x_table(direction):
    line = np.arange(HALF)
    angle = 2 * np.pi / HALF * (line[:, None] * line[None, :] % HALF)
    both = np.eye(2)
    cosine, sine = np.kron(both, np.cos(angle)), direction * np.kron(both, np.sin(angle))
    return two_parts(np.block([[cosine, sine], [-sine, cosine]]))


def y_twist():
    angle = 2 * np.pi / N * (np.arange(16)[:, None] * np.arange(LANES)[None, :] % N)
    return np.stack([np.cos(angle), np.sin(angle)]).astype(np.float32)


def x_twist():
    column = np.arange(LANES) % HALF
    angle = 2 * np.pi / N * (np.arange(FFT)[:, None] * column[None, :] % N)
    table = np.stack([np.cos(angle), np.sin(angle)]).astype(np.float32)
    return np.broadcast_to(table[:, :, None, :], (2, FFT, 8, LANES)).copy()


def split(values):
    high = values.astype(BF16)
    return high, (values - high.astype(F32)).astype(BF16)


def dot(left, right, dims):
    return lax.dot_general(left, right, (dims, ((), ())), preferred_element_type=F32)


def product(left, right, dims):
    (left_high, left_low), (right_high, right_low) = left, right
    return dot(left_high, right_high, dims) + (dot(left_low, right_high, dims) + dot(left_high, right_low, dims))


def turn(value, part, whole, direction):
    real, imag = value
    part = part % whole
    eighth = 8 * part
    if eighth % whole == 0:
        eighth = eighth // whole
        root = math.sqrt(0.5)
        if eighth == 0:
            return value
        if eighth == 4:
            return (-real, -imag)
        if eighth == 2 or eighth == 6:
            return (-imag, real) if (eighth == 2) == (direction > 0) else (imag, -real)
    cosine, sine = math.cos(2 * math.pi * part / whole), direction * math.sin(2 * math.pi * part / whole)
    return (real * cosine - imag * sine, real * sine + imag * cosine)


def plus(left, right):
    return (left[0] + right[0], left[1] + right[1])


def minus(left, right):
    return (left[0] - right[0], left[1] - right[1])


def small_dft(values, direction):
    size = len(values)
    if size == 1:
        return values
    even = small_dft(values[0::2], direction)
    odd = small_dft(values[1::2], direction)
    odd = [turn(odd[index], index, size, direction) for index in range(size // 2)]
    return [plus(even[index], odd[index]) for index in range(size // 2)] + [
        minus(even[index], odd[index]) for index in range(size // 2)
    ]


def dft32(real, imag, direction):
    shape = (4, 8) + real.shape[1:]
    real, imag = real.reshape(shape), imag.reshape(shape)
    first = small_dft([(real[u], imag[u]) for u in range(4)], direction)
    second = []
    for v in range(8):
        turned = [turn((first[w][0][v], first[w][1][v]), w * v, 32, direction) for w in range(4)]
        second.append((jnp.stack([value[0] for value in turned]), jnp.stack([value[1] for value in turned])))
    done = small_dft(second, direction)
    flat = (32,) + real.shape[2:]
    return (
        jnp.stack([value[0] for value in done]).reshape(flat),
        jnp.stack([value[1] for value in done]).reshape(flat),
    )


def real_dft(values):
    size = len(values)
    if size == 2:
        return [values[0] + values[1], values[0] - values[1]]
    even, odd = real_dft(values[0::2]), real_dft(values[1::2])
    half, quarter = size // 2, size // 4
    out = [None] * (half + 1)
    out[0], out[half] = even[0] + odd[0], even[0] - odd[0]
    out[quarter] = (even[quarter], -odd[quarter])
    for index in range(1, quarter):
        turned = turn(odd[index], index, size, -1)
        out[index] = plus(even[index], turned)
        back = minus(even[index], turned)
        out[half - index] = (back[0], -back[1])
    return out


def real_inverse(values):
    half = len(values) - 1
    size = 2 * half
    if size == 2:
        return [values[0] + values[1], values[0] - values[1]]
    quarter = size // 4
    even, odd = [None] * (quarter + 1), [None] * (quarter + 1)
    even[0], odd[0] = values[0] + values[half], values[0] - values[half]
    even[quarter], odd[quarter] = 2.0 * values[quarter][0], -2.0 * values[quarter][1]
    for index in range(1, quarter):
        mirror = (values[half - index][0], -values[half - index][1])
        even[index] = plus(values[index], mirror)
        odd[index] = turn(minus(values[index], mirror), index, size, 1)
    out = [None] * size
    out[0::2], out[1::2] = real_inverse(even), real_inverse(odd)
    return out


def y_operands(field, twist_cos, twist_sin):
    parts = real_dft([field[:, LANES * index : LANES * (index + 1)] for index in range(16)])
    sign = 1.0 - 2.0 * (lax.broadcasted_iota(jnp.int32, (OWN, LANES), 1) % 2).astype(F32)

    def twisted(index):
        cosine, sine = twist_cos[index][None, :], twist_sin[index][None, :]
        if index == 8:
            return jnp.concatenate([parts[8] * cosine, -parts[8] * sine], 1)
        real, imag = parts[index]
        return jnp.concatenate([real * cosine + imag * sine, imag * cosine - real * sine], 1)

    signs = jnp.concatenate([sign, sign], 1)
    out = [jnp.concatenate([jnp.concatenate([parts[0], jnp.zeros_like(parts[0])], 1), twisted(8)], 0)]
    for index in range(1, 8):
        value = twisted(index)
        out.append(jnp.concatenate([value, value * signs], 0))
    return out


def y_result(sums, twist_cos, twist_sin):
    sign = 1.0 - 2.0 * (lax.broadcasted_iota(jnp.int32, (OWN, LANES), 1) % 2).astype(F32)
    values = [sums[0][:OWN, 2 * LANES :]]
    for index in range(1, 8):
        real = sums[index][:OWN, :LANES] + sign * sums[index][OWN:, :LANES]
        imag = sums[index][:OWN, LANES:] + sign * sums[index][OWN:, LANES:]
        cosine, sine = twist_cos[index][None, :], twist_sin[index][None, :]
        values.append((real * cosine - imag * sine, real * sine + imag * cosine))
    real, imag = sums[0][OWN:, :LANES], sums[0][OWN:, LANES : 2 * LANES]
    values.append(2.0 * (real * twist_cos[8][None, :] - imag * twist_sin[8][None, :]))
    return jnp.concatenate([jnp.clip(value, -1.0, 1.0) for value in real_inverse(values)], 1)


def x_forward(real, imag, table, twist_cos, twist_sin):
    real, imag = dft32(real, imag, -1)
    both = jnp.concatenate([real * twist_cos + imag * twist_sin, imag * twist_cos - real * twist_sin], 2)
    out = product(split(both.reshape(256, 256)), table, ((1,), (0,)))
    return out.reshape(FFT, 8, 2 * LANES)


def x_inverse(values, table, twist_cos, twist_sin):
    out = product(split(values.reshape(256, 256)), table, ((1,), (0,))).reshape(FFT, 8, 2 * LANES)
    real, imag = out[:, :, :LANES], out[:, :, LANES:]
    return dft32(real * twist_cos - imag * twist_sin, real * twist_sin + imag * twist_cos, 1)


SEND, RECV, POWER, MEAN, BACK = range(5)


def kernel(
    field_hbm, yf_hbm, yi_hbm, xf_hbm, xi_hbm, yt_hbm, xt_hbm, xs_hbm, y_shape,
    out_hbm,
    field, yf, yi, xf, xi, yt, xt, xs, out,
    sent, received, spec, power, powers, root, bound, back, returned, sym,
    load_sem, send_sem, recv_sem,
):
    me = lax.axis_index("fft")
    plane = lax.axis_index("plane")
    special = me == 0

    barrier = pltpu.get_barrier_semaphore()

    def fft_peer(step):
        return lax.rem(me + step, FFT)

    def plane_peer(step):
        return lax.rem(plane + step, PLANES)

    loads = []
    for index, (source, target) in enumerate(
        [(field_hbm, field), (yf_hbm, yf), (yt_hbm, yt), (xf_hbm, xf), (xt_hbm, xt), (xs_hbm, xs), (xi_hbm, xi), (yi_hbm, yi)]
    ):
        copy = pltpu.make_async_copy(source, target, load_sem.at[index])
        copy.start()
        loads.append(copy)

    @pl.loop(1, FFT)
    def _(step):
        pl.semaphore_signal(barrier, inc=1, device_id=(fft_peer(step), plane), device_id_type=MESH)

    @pl.loop(1, PLANES)
    def _(step):
        pl.semaphore_signal(barrier, inc=1, device_id=(me, plane_peer(step)), device_id_type=MESH)

    for copy in loads[:3]:
        copy.wait()
    operands = [split(value) for value in y_operands(field[:, 0, :], yt[0], yt[1])]
    for index, operand in enumerate(operands):
        done = product((yf[0, :128], yf[1, :128]), operand, ((1,), (1,)))
        if index == 0:
            extra = product((yf[0, 128:], yf[1, 128:]), operand, ((1,), (1,)))[0:1, :]
            row = lax.broadcasted_iota(jnp.int32, (128, LANES), 0)
            lane = lax.broadcasted_iota(jnp.int32, (128, LANES), 1)
            done = jnp.where((row == 8) & (lane < HALF), extra, done)
        sent[:, 4 * index : 4 * index + 4] = done.reshape(2, 4, 16, LANES)
    for chunk in range(CHUNKS):
        received[chunk, me] = sent[chunk, me]

    pl.semaphore_wait(barrier, FFT - 1 + PLANES - 1)

    def all_to_all(source, target, chunk, kind):
        @pl.loop(1, FFT)
        def _(step):
            peer = fft_peer(step)
            pltpu.make_async_remote_copy(
                src_ref=source.at[chunk, peer],
                dst_ref=target.at[chunk, me],
                send_sem=send_sem.at[kind, chunk],
                recv_sem=recv_sem.at[kind, chunk],
                device_id=(peer, plane),
                device_id_type=MESH,
            ).start()

    def to_planes(source, target, chunk, kind):
        @pl.loop(1, PLANES)
        def _(step):
            peer = plane_peer(step)
            pltpu.make_async_remote_copy(
                src_ref=source(peer),
                dst_ref=target,
                send_sem=send_sem.at[kind, chunk],
                recv_sem=recv_sem.at[kind, chunk],
                device_id=(me, peer),
                device_id_type=MESH,
            ).start()

    def wait_for(ref, sem):
        pltpu.make_async_copy(ref, ref, sem).wait()

    all_to_all(sent, received, 0, SEND)
    all_to_all(sent, received, 1, SEND)

    for copy in loads[3:]:
        copy.wait()
    group, block = me // 4, lax.rem(me, 4)
    row = lax.broadcasted_iota(jnp.int32, (8, LANES), 0)
    lane = lax.broadcasted_iota(jnp.int32, (8, LANES), 1)
    for chunk in range(CHUNKS):
        here, other = jnp.zeros((8, LANES), F32), jnp.zeros((8, LANES), F32)
        for half in range(2):
            for step in range(8):
                line = 16 * block + 8 * chunk + step
                ky = jnp.where(group == 0, 8 * half + 16 * line, group + 16 * (line + 64 * half))
                place = (row == step) & (lane // HALF == half)
                here = jnp.where(place, y_shape[ky], here)
                other = jnp.where(place, y_shape[lax.rem(N - ky, N)], other)
        bound[0, chunk] = here[None] * xs[0]
        bound[1, chunk] = other[None] * xs[1]

    @pl.when(special)
    def _():
        here = jnp.where(lane < HALF, y_shape[0], y_shape[N // 2])
        bound[0, 2] = here[None] * xs[0]
        bound[1, 2] = here[None] * xs[1]

    def along_x(real, imag, chunk):
        done = x_forward(real, imag, (xf[0], xf[1]), xt[0], xt[1])
        spec[chunk] = done
        real, imag = done[:, :, :LANES], done[:, :, LANES:]
        power[chunk] = real * real + imag * imag
        mine = pl.ds(2 * plane, 2)
        powers[chunk, plane] = power[chunk, mine]
        to_planes(lambda peer: power.at[chunk, pl.ds(2 * peer, 2)], powers.at[chunk, plane], chunk, POWER)

    def average(chunk):
        wait_for(powers.at[chunk, pl.ds(0, PLANES - 1)], recv_sem.at[POWER, chunk])
        mine = pl.ds(2 * plane, 2)
        total = powers[chunk, 0]
        for index in range(1, PLANES):
            total = total + powers[chunk, index]
        root[chunk, mine] = jnp.sqrt(total * (1.0 / PLANES))
        to_planes(lambda peer: root.at[chunk, mine], root.at[chunk, mine], chunk, MEAN)

    def clipped(chunk):
        wait_for(root.at[chunk, pl.ds(0, 2 * (PLANES - 1))], recv_sem.at[MEAN, chunk])
        here, other = bound[0, chunk] * root[chunk], bound[1, chunk] * root[chunk]
        real, imag = spec[chunk, :, :, :LANES], spec[chunk, :, :, LANES:]
        return [
            0.5 * (jnp.clip(value, -here, here) + jnp.clip(value, -other, other)) for value in (real, imag)
        ]

    def first_half(chunk):
        wait_for(received.at[chunk, pl.ds(0, FFT - 1)], recv_sem.at[SEND, chunk])
        along_x(received[chunk, :, :8], received[chunk, :, 8:], chunk)

    def second_half(chunk):
        real, imag = clipped(chunk)
        sym[:, :, :LANES] = real
        sym[:, :, LANES:] = imag
        if chunk == 0:

            @pl.when(special)
            def _():
                real, imag = clipped(2)
                shape = (FFT, 8, LANES)
                place = (lax.broadcasted_iota(jnp.int32, shape, 1) == 0) & (
                    lax.broadcasted_iota(jnp.int32, shape, 2) < HALF
                )
                sym[:, :, :LANES] = jnp.where(place, real - pltpu.roll(imag, HALF, 2), sym[:, :, :LANES])
                sym[:, :, LANES:] = jnp.where(place, imag + pltpu.roll(real, HALF, 2), sym[:, :, LANES:])

        real, imag = x_inverse(sym[...], (xi[0], xi[1]), xt[0], xt[1])
        back[chunk, :, :8] = real
        back[chunk, :, 8:] = imag
        returned[chunk, me] = back[chunk, me]
        all_to_all(back, returned, chunk, BACK)

    first_half(0)

    @pl.when(special)
    def _():
        real, imag = received[0, :, :8], received[0, :, 8:]
        halves = lax.broadcasted_iota(jnp.int32, real.shape, 2) < HALF
        along_x(jnp.where(halves, real, pltpu.roll(imag, HALF, 2)), jnp.zeros_like(real), 2)

    average(0)

    @pl.when(special)
    def _():
        average(2)

    first_half(1)
    second_half(0)
    average(1)
    second_half(1)

    for chunk in range(CHUNKS):
        wait_for(returned.at[chunk, pl.ds(0, FFT - 1)], recv_sem.at[BACK, chunk])
    sums = []
    for index in range(8):
        rows = jnp.concatenate([returned[chunk, 4 * index : 4 * index + 4].reshape(64, LANES) for chunk in range(CHUNKS)], 0)
        width = 2 * LANES if index else 3 * LANES
        sums.append(product(split(rows), (yi[0, :, :width], yi[1, :, :width]), ((0,), (0,))))
    out[:, 0, :] = y_result(sums, yt[0], yt[1])
    store = pltpu.make_async_copy(out, out_hbm, load_sem.at[0])
    store.start()

    for chunk in range(CHUNKS):
        for kind in (SEND, BACK):
            wait_for(received.at[chunk, pl.ds(0, FFT - 1)], send_sem.at[kind, chunk])
        for kind in (POWER, MEAN):
            wait_for(powers.at[chunk, pl.ds(0, PLANES - 1)], send_sem.at[kind, chunk])

    @pl.when(special)
    def _():
        for kind in (POWER, MEAN):
            wait_for(powers.at[2, pl.ds(0, PLANES - 1)], send_sem.at[kind, 2])

    store.wait()


def correct(error_field, x_shape, y_shape):
    shape = error_field.shape
    factors = jnp.stack([x_shape, jnp.roll(x_shape[::-1], 1)]).reshape(2, HALF, FFT).transpose(0, 2, 1)
    factors = jnp.broadcast_to(factors[:, :, None, None, :], (2, FFT, 8, 2, HALF)).reshape(2, FFT, 8, LANES)
    operands = [
        error_field, y_forward_table(), y_inverse_table(), x_table(-1), x_table(1), y_twist(), x_twist(), factors,
    ]
    operands = [jnp.asarray(operand) for operand in operands]
    anywhere = pl.BlockSpec(memory_space=pl.ANY)
    return pl.pallas_call(
        kernel,
        out_shape=jax.ShapeDtypeStruct(shape, F32),
        in_specs=[anywhere] * 8 + [pl.BlockSpec(memory_space=pltpu.SMEM)],
        out_specs=anywhere,
        scratch_shapes=[pltpu.VMEM(operand.shape, operand.dtype) for operand in operands]
        + [
            pltpu.VMEM(shape, F32),
            pltpu.VMEM((CHUNKS, FFT, 16, LANES), F32),
            pltpu.VMEM((CHUNKS, FFT, 16, LANES), F32),
            pltpu.VMEM((CHUNKS + 1, FFT, 8, 2 * LANES), F32),
            pltpu.VMEM((CHUNKS + 1, FFT, 8, LANES), F32),
            pltpu.VMEM((CHUNKS + 1, PLANES, 2, 8, LANES), F32),
            pltpu.VMEM((CHUNKS + 1, FFT, 8, LANES), F32),
            pltpu.VMEM((2, CHUNKS + 1, FFT, 8, LANES), F32),
            pltpu.VMEM((CHUNKS, FFT, 16, LANES), F32),
            pltpu.VMEM((CHUNKS, FFT, 16, LANES), F32),
            pltpu.VMEM((FFT, 8, 2 * LANES), F32),
            pltpu.SemaphoreType.DMA((8,)),
            pltpu.SemaphoreType.DMA((5, CHUNKS + 1)),
            pltpu.SemaphoreType.DMA((5, CHUNKS + 1)),
        ],
        compiler_params=pltpu.CompilerParams(
            collective_id=0, has_side_effects=True, vmem_limit_bytes=48 * 1024 * 1024
        ),
    )(*operands, y_shape)


def solution(mesh):
    placed = (P("fft", "plane", None), P(), P())
    return jax.shard_map(
        correct, mesh=mesh, in_specs=placed, out_specs=P("fft", "plane", None), check_vma=False
    )
```

profile of v0, /device:TPU:1, one launch (start us, length us, event | category | flops | bytes accessed | tf_op | source)
XLA Modules:
  0.0 70.9 jit_solution(1115355672300670106)
XLA Ops:
  0.0 0.0 copy-start
  0.0 1.3 %slice.12 = f32[1]{0:T(128)} slice(f32[2048]{0:T(1024)} %param.10), slice={[0:1]} | slice | bytes 8 | tf_op jit(solution)/shard_map/jit(_roll_static)/slice | solution.py:433
  1.3 0.8 %slice.13 = f32[2047]{0:T(1024)S(1)} slice(f32[2048]{0:T(1024)} %param.10), slice={[1:2048]} | slice | bytes 16376 | tf_op jit(solution)/shard_map/jit(_roll_static)/slice | solution.py:433
  2.0 0.1 reverse.2
  2.1 0.1 slice.15
  2.2 0.7 %pad_maximum_fusion = f32[2048]{0:T(1024)S(1)} fusion(f32[2047]{0:T(1024)S(1)} %slice.15, f32[1]{0:T(128)} %slice.12), kind=kLoop, calls=%fused_computation.1 | loop fusion | flops 2048 | bytes 16384 | tf_op jit(solution)/shard_map/jit(_roll_static)/concatenate | solution.py:433
  2.9 0.1 stack.10
  3.0 0.8 %stack.9 = f32[1,64,32]{2,1,0:T(8,128)S(1)} reshape(f32[2048]{0:T(1024)} %param.10) | data formatting | bytes 16384 | tf_op jit(solution)/shard_map/stack | solution.py:433
  3.8 0.1 copy.10
  3.8 0.0 copy-start.1
  3.9 0.1 broadcast_in_dim.11
  4.0 0.0 copy-start.6
  4.0 0.0 copy-start.7
  4.0 0.0 copy-done
  4.0 0.8 %copy-done.1 = f32[2,32,8,128]{3,2,1,0:T(8,128)S(1)} copy-done((f32[2,32,8,128]{3,2,1,0:T(8,128)S(1)}, f32[2,32,8,128]{3,2,1,0:T(8,128)}, u32[]{:S(2)}) %copy-start.1) | copy-done | bytes 262168
  4.8 0.0 copy-done.6
  4.8 0.0 copy-done.7
  4.8 0.0 copy-start.2
  4.8 0.9 %copy-done.2 = bf16[2,256,256]{2,1,0:T(8,128)(2,1)S(1)} copy-done((bf16[2,256,256]{2,1,0:T(8,128)(2,1)S(1)}, bf16[2,256,256]{2,1,0:T(8,128)(2,1)}, u32[]{:S(2)}) %copy-start.2) | copy-done | bytes 262168
  5.7 0.0 copy-start.3
  5.8 0.9 %copy-done.3 = bf16[2,256,256]{2,1,0:T(8,128)(2,1)S(1)} copy-done((bf16[2,256,256]{2,1,0:T(8,128)(2,1)S(1)}, bf16[2,256,256]{2,1,0:T(8,128)(2,1)}, u32[]{:S(2)}) %copy-start.3) | copy-done | bytes 262168
  6.7 0.0 copy-start.4
  6.7 0.9 %copy-done.4 = bf16[2,128,384]{2,1,0:T(8,128)(2,1)S(1)} copy-done((bf16[2,128,384]{2,1,0:T(8,128)(2,1)S(1)}, bf16[2,128,384]{2,1,0:T(8,128)(2,1)}, u32[]{:S(2)}) %copy-start.4) | copy-done | bytes 196632
  7.6 0.0 copy-start.5
  7.6 0.9 %copy-done.5 = bf16[2,144,256]{2,1,0:T(8,128)(2,1)S(1)} copy-done((bf16[2,144,256]{2,1,0:T(8,128)(2,1)S(1)}, bf16[2,144,256]{2,1,0:T(8,128)(2,1)}, u32[]{:S(2)}) %copy-start.5) | copy-done | bytes 147480
  8.5 61.6 %shard_map.91 = f32[64,1,2048]{2,1,0:T(1,128)S(1)} custom-call(f32[64,1,2048]{2,1,0:T(1,128)S(1)} %copy-done, bf16[2,144,256]{2,1,0:T(8,128)(2,1)S(1)} %copy-done.5, bf16[2,128,384]{2,1,0:T(8,128)(2,1)S(1)} %copy-done.4, bf16[2,256,256]{2,1,0:T(8,128)(2,1)S(1)} %copy-done.3, bf16[2,256,256]{2,1,0:T(8,128)(2,1)S(1)} %copy-done.2, ...), custom_call_target="tpu_custom_call" | custom-call | tf_op jit(solution)/shard_map/pallas_call | solution.py:440
  70.1 0.8 %copy.12 = f32[64,1,2048]{2,1,0:T(1,128)} copy(f32[64,1,2048]{2,1,0:T(1,128)S(1)} %shard_map.91) | data formatting | bytes 1048576
  (3 shorter events, 0.1 us)
Async XLA Ops:
  0.0 4.0 %copy-start = (f32[64,1,2048]{2,1,0:T(1,128)S(1)}, f32[64,1,2048]{2,1,0:T(1,128)}, u32[]{:S(2)}) copy-start(f32[64,1,2048]{2,1,0:T(1,128)} %field_hbm.1) | copy-start | bytes 1572868
  3.8 1.0 %copy-start.1 = (f32[2,32,8,128]{3,2,1,0:T(8,128)S(1)}, f32[2,32,8,128]{3,2,1,0:T(8,128)}, u32[]{:S(2)}) copy-start(f32[2,32,8,128]{3,2,1,0:T(8,128)} %constant.17.clone.xt_hbm) | copy-start | bytes 786436
  4.0 0.8 %copy-start.6 = (f32[2,16,128]{2,1,0:T(8,128)S(1)}, f32[2,16,128]{2,1,0:T(8,128)}, u32[]{:S(2)}) copy-start(f32[2,16,128]{2,1,0:T(8,128)} %constant.16.clone.yt_hbm) | copy-start | bytes 49156
  4.0 0.8 %copy-start.7 = (f32[2048]{0:T(1024)S(1)}, f32[2048]{0:T(1024)}, u32[]{:S(2)}) copy-start(f32[2048]{0:T(1024)} %y_shape.1) | copy-start | bytes 24580
  4.8 1.0 %copy-start.2 = (bf16[2,256,256]{2,1,0:T(8,128)(2,1)S(1)}, bf16[2,256,256]{2,1,0:T(8,128)(2,1)}, u32[]{:S(2)}) copy-start(bf16[2,256,256]{2,1,0:T(8,128)(2,1)} %constant.15.clone.xi_hbm) | copy-start | bytes 786436
  5.7 0.9 %copy-start.3 = (bf16[2,256,256]{2,1,0:T(8,128)(2,1)S(1)}, bf16[2,256,256]{2,1,0:T(8,128)(2,1)}, u32[]{:S(2)}) copy-start(bf16[2,256,256]{2,1,0:T(8,128)(2,1)} %constant.14.clone.xf_hbm) | copy-start | bytes 786436
  6.7 0.9 %copy-start.4 = (bf16[2,128,384]{2,1,0:T(8,128)(2,1)S(1)}, bf16[2,128,384]{2,1,0:T(8,128)(2,1)}, u32[]{:S(2)}) copy-start(bf16[2,128,384]{2,1,0:T(8,128)(2,1)} %constant.13.clone.yi_hbm) | copy-start | bytes 589828
  7.6 0.9 %copy-start.5 = (bf16[2,144,256]{2,1,0:T(8,128)(2,1)S(1)}, bf16[2,144,256]{2,1,0:T(8,128)(2,1)}, u32[]{:S(2)}) copy-start(bf16[2,144,256]{2,1,0:T(8,128)(2,1)} %constant.12.clone.yf_hbm) | copy-start | bytes 442372
where the time goes:
time: 71.3 us; the launch traced here: 70.9 us
  Pallas kernels  61.6 us (86%)
  local copies, waits for them, and re-layouts  8.56 us (12%)
  other arithmetic  0.73 us (1%)
    pallas_call x1, Pallas kernels, correct(): pl.pallas_call(kernel, out_shape=jax.ShapeDtypeStruct(shape, F32), in_spe...  61.6 us
    unnamed x19, local copies, waits for them, and re-layouts  5.48 us
    slice x2, local copies, waits for them, and re-layouts, correct(): jnp.roll(x_shape[::-1], 1)  2.02 us

commit v1 on v0

v1 whole, which is shorter than its diff:
```python
import math

import jax
import jax.numpy as jnp
import ml_dtypes
import numpy as np
from jax import lax
from jax.experimental import pallas as pl
from jax.experimental.pallas import tpu as pltpu
from jax.sharding import PartitionSpec as P

F32 = jnp.float32
BF16 = jnp.bfloat16
N = 2048
FFT = 32
PLANES = 16
OWN = N // FFT
HALF = 64
LANES = 128
CHUNKS = 4
SPECIAL = CHUNKS
MESH = pl.DeviceIdType.MESH


def two_parts(table):
    table = np.asarray(table, np.float64)
    high = table.astype(np.float32).astype(ml_dtypes.bfloat16)
    low = (table - high.astype(np.float64)).astype(np.float32).astype(ml_dtypes.bfloat16)
    return np.stack([high, low])


def row_order():
    block, part, step = np.meshgrid(np.arange(16), np.arange(2), np.arange(4), indexing="ij")
    return part.reshape(-1), (block * 4 + step).reshape(-1)


def y_forward_table():
    part, row = row_order()
    angle = 2 * np.pi / LANES * (row[:, None] * np.arange(LANES)[None, :] % LANES)
    cosine, sine = np.cos(angle), np.sin(angle)
    part = part[:, None]
    table = np.concatenate([np.where(part == 0, cosine, -sine), np.where(part == 0, sine, cosine)], 1)
    extra = np.zeros((16, 2 * LANES))
    extra[0, :LANES] = 1 - 2 * (np.arange(LANES) % 2)
    return two_parts(np.concatenate([table, extra], 0))


def y_inverse_table():
    part, row = row_order()
    column = np.arange(LANES)
    angle = 2 * np.pi / LANES * (row[:, None] * column[None, :] % LANES)
    cosine, sine = np.cos(angle), np.sin(angle)
    part, row = part[:, None], row[:, None]
    plain = np.concatenate([np.where(part == 0, cosine, -sine), np.where(part == 0, sine, cosine)], 1)
    sign = (1 - 2 * (column % 2))[None, :]
    first = np.where(part == 0, np.where(row == 0, 1.0, 2 * cosine), np.where(row == 0, sign, -2 * sine))
    return two_parts(np.concatenate([plain, first], 1) / (N * N))


def x_table(direction):
    line = np.arange(HALF)
    angle = 2 * np.pi / HALF * (line[:, None] * line[None, :] % HALF)
    both = np.eye(2)
    cosine, sine = np.kron(both, np.cos(angle)), direction * np.kron(both, np.sin(angle))
    return two_parts(np.block([[cosine, sine], [-sine, cosine]]))


def y_twist():
    angle = 2 * np.pi / N * (np.arange(16)[:, None] * np.arange(LANES)[None, :] % N)
    return np.stack([np.cos(angle), np.sin(angle)]).astype(np.float32)


def x_twist():
    half = np.arange(8)[None, :, None] // 4
    line = np.arange(16)[:, None, None]
    column = np.arange(LANES)[None, None, :] % HALF
    inner = 2 * np.pi / FFT * (half * line % FFT) * np.ones_like(column)
    outer = 2 * np.pi / N * ((2 * line + half) * column % N)
    return np.stack([np.cos(inner), np.sin(inner), np.cos(outer), np.sin(outer)]).astype(np.float32)


def x_choices():
    pick, spread = np.zeros((2, 5, FFT, LANES)), np.zeros((2, 5, 16, LANES))
    for sign in range(2):
        for p in range(FFT):
            for q in range(HALF):
                kx = p + FFT * q if sign == 0 else (N - p - FFT * q) % N
                case = 4 if sign == 1 and p == 0 and q % 4 == 0 else q % 4
                pick[sign, case, p % 2 * 16 + p // 2, kx % LANES] = 1
                spread[sign, case, kx // LANES, [q, HALF + q]] = 1
    return pick.reshape(2 * 5 * FFT, LANES).astype(ml_dtypes.bfloat16), spread.astype(ml_dtypes.bfloat16)


def split(values):
    high = values.astype(BF16)
    return high, (values - high.astype(F32)).astype(BF16)


def dot(left, right, dims):
    return lax.dot_general(left, right, (dims, ((), ())), preferred_element_type=F32)


def product(left, right, dims):
    (left_high, left_low), (right_high, right_low) = left, right
    return dot(left_high, right_high, dims) + (dot(left_low, right_high, dims) + dot(left_high, right_low, dims))


def turn(value, part, whole, direction):
    real, imag = value
    part = part % whole
    eighth = 8 * part
    if eighth % whole == 0:
        eighth = eighth // whole
        root = math.sqrt(0.5)
        if eighth == 0:
            return value
        if eighth == 4:
            return (-real, -imag)
        if eighth == 2 or eighth == 6:
            return (-imag, real) if (eighth == 2) == (direction > 0) else (imag, -real)
    cosine, sine = math.cos(2 * math.pi * part / whole), direction * math.sin(2 * math.pi * part / whole)
    return (real * cosine - imag * sine, real * sine + imag * cosine)


def plus(left, right):
    return (left[0] + right[0], left[1] + right[1])


def minus(left, right):
    return (left[0] - right[0], left[1] - right[1])


def small_dft(values, direction):
    size = len(values)
    if size == 1:
        return values
    even = small_dft(values[0::2], direction)
    odd = small_dft(values[1::2], direction)
    odd = [turn(odd[index], index, size, direction) for index in range(size // 2)]
    return [plus(even[index], odd[index]) for index in range(size // 2)] + [
        minus(even[index], odd[index]) for index in range(size // 2)
    ]


def dft16(real, imag, direction):
    shape = (4, 4) + real.shape[1:]
    real, imag = real.reshape(shape), imag.reshape(shape)
    first = small_dft([(real[u], imag[u]) for u in range(4)], direction)
    second = []
    for v in range(4):
        turned = [turn((first[w][0][v], first[w][1][v]), w * v, 16, direction) for w in range(4)]
        second.append((jnp.stack([value[0] for value in turned]), jnp.stack([value[1] for value in turned])))
    done = small_dft(second, direction)
    flat = (16,) + real.shape[2:]
    return (
        jnp.stack([value[0] for value in done]).reshape(flat),
        jnp.stack([value[1] for value in done]).reshape(flat),
    )


def real_dft(values):
    size = len(values)
    if size == 2:
        return [values[0] + values[1], values[0] - values[1]]
    even, odd = real_dft(values[0::2]), real_dft(values[1::2])
    half, quarter = size // 2, size // 4
    out = [None] * (half + 1)
    out[0], out[half] = even[0] + odd[0], even[0] - odd[0]
    out[quarter] = (even[quarter], -odd[quarter])
    for index in range(1, quarter):
        turned = turn(odd[index], index, size, -1)
        out[index] = plus(even[index], turned)
        back = minus(even[index], turned)
        out[half - index] = (back[0], -back[1])
    return out


def real_inverse(values):
    half = len(values) - 1
    size = 2 * half
    if size == 2:
        return [values[0] + values[1], values[0] - values[1]]
    quarter = size // 4
    even, odd = [None] * (quarter + 1), [None] * (quarter + 1)
    even[0], odd[0] = values[0] + values[half], values[0] - values[half]
    even[quarter], odd[quarter] = 2.0 * values[quarter][0], -2.0 * values[quarter][1]
    for index in range(1, quarter):
        mirror = (values[half - index][0], -values[half - index][1])
        even[index] = plus(values[index], mirror)
        odd[index] = turn(minus(values[index], mirror), index, size, 1)
    out = [None] * size
    out[0::2], out[1::2] = real_inverse(even), real_inverse(odd)
    return out


def y_operands(field, twist_cos, twist_sin):
    parts = real_dft([field[:, LANES * index : LANES * (index + 1)] for index in range(16)])
    sign = 1.0 - 2.0 * (lax.broadcasted_iota(jnp.int32, (OWN, LANES), 1) % 2).astype(F32)

    def twisted(index):
        cosine, sine = twist_cos[index][None, :], twist_sin[index][None, :]
        if index == 8:
            return jnp.concatenate([parts[8] * cosine, -parts[8] * sine], 1)
        real, imag = parts[index]
        return jnp.concatenate([real * cosine + imag * sine, imag * cosine - real * sine], 1)

    signs = jnp.concatenate([sign, sign], 1)
    out = [jnp.concatenate([jnp.concatenate([parts[0], jnp.zeros_like(parts[0])], 1), twisted(8)], 0)]
    for index in range(1, 8):
        value = twisted(index)
        out.append(jnp.concatenate([value, value * signs], 0))
    return out


def y_line(total, index, twist_cos, twist_sin):
    if index == 0:
        real, imag = total[OWN:, :LANES], total[OWN:, LANES : 2 * LANES]
        return total[:OWN, 2 * LANES :], 2.0 * (real * twist_cos[8][None, :] - imag * twist_sin[8][None, :])
    sign = 1.0 - 2.0 * (lax.broadcasted_iota(jnp.int32, (OWN, LANES), 1) % 2).astype(F32)
    real = total[:OWN, :LANES] + sign * total[OWN:, :LANES]
    imag = total[:OWN, LANES:] + sign * total[OWN:, LANES:]
    cosine, sine = twist_cos[index][None, :], twist_sin[index][None, :]
    return real * cosine - imag * sine, real * sine + imag * cosine


def y_result(lines):
    values = real_inverse([lines[0][0], *lines[1:], lines[0][1]])
    return [jnp.clip(value, -1.0, 1.0) for value in values]


def upper(shape):
    return lax.broadcasted_iota(jnp.int32, shape, 1) < 4


def x_forward(blocks, table, twist):
    total, rest = blocks[:16] + blocks[16:], blocks[:16] - blocks[16:]
    top = upper(total.shape)
    real = jnp.where(top, total, pltpu.roll(rest, 4, 1))
    imag = jnp.where(top, pltpu.roll(total, 4, 1), rest)
    real, imag = real * twist[0] + imag * twist[1], imag * twist[0] - real * twist[1]
    real, imag = dft16(real, imag, -1)
    both = jnp.concatenate([real * twist[2] + imag * twist[3], imag * twist[2] - real * twist[3]], 2)
    return product(split(both.reshape(LANES, 2 * LANES)), table, ((1,), (0,))).reshape(16, 8, 2 * LANES)


def x_inverse(values, table, twist):
    out = product(split(values.reshape(LANES, 2 * LANES)), table, ((1,), (0,))).reshape(16, 8, 2 * LANES)
    real, imag = out[:, :, :LANES], out[:, :, LANES:]
    real, imag = dft16(real * twist[2] - imag * twist[3], real * twist[3] + imag * twist[2], 1)
    real, imag = real * twist[0] - imag * twist[1], real * twist[1] + imag * twist[0]
    top = upper(real.shape)
    even = jnp.where(top, real, pltpu.roll(imag, 4, 1))
    odd = jnp.where(top, pltpu.roll(real, 4, 1), imag)
    return jnp.concatenate([even + odd, even - odd], 0)


def x_factors(shape, pick, spread):
    rest, parts = shape, []
    for _ in range(3):
        part = rest.astype(BF16)
        parts.append(part)
        rest = rest - part.astype(F32)
    chosen = [dot(pick, part, ((1,), (1,))).astype(BF16) for part in parts]
    out = []
    for sign in range(2):
        total = None
        for part in reversed(chosen):
            for case in range(4 + sign):
                start = FFT * (5 * sign + case)
                value = dot(part[start : start + FFT], spread[sign, case], ((1,), (0,)))
                total = value if total is None else total + value
        even, odd = total[:16, None, :], total[16:, None, :]
        out.append(jnp.where(upper((16, 8, LANES)), even, odd))
    return out


SEND, POWER, MEAN, BACK = range(4)


def far_first(step):
    return lax.rem(12 + (step + 1) // 2 * (1 - 2 * lax.rem(step, 2)), 8)


def kernel(
    field_hbm, yf_hbm, yi_hbm, xf_hbm, xi_hbm, yt_hbm, xt_hbm, pick_hbm, spread_hbm, xs_hbm, ys_hbm,
    out_hbm,
    field, yf, yi, xf, xi, yt, xt, pick, spread, xs, y_shape, out,
    sent, received, spec, power, powers, root, bound, back, returned, sym, lines,
    load_sem, send_sem, recv_sem,
):
    me = lax.axis_index("fft")
    plane = lax.axis_index("plane")
    other = plane + 1 - 2 * lax.rem(plane, 2)
    special = me == 0
    barrier = pltpu.get_barrier_semaphore()

    def fft_peer(step):
        return lax.rem(me // 4 + far_first(lax.rem(step, 8)), 8) * 4 + lax.rem(lax.rem(me, 4) + 1 + step // 8, 4)

    def plane_peer(step):
        return lax.rem(plane // 2 + far_first(step // 2), 8) * 2 + lax.rem(plane + 1 + step, 2)

    loads = []
    for index, (source, target) in enumerate(
        [
            (field_hbm, field), (yt_hbm, yt), (yf_hbm, yf), (ys_hbm, y_shape), (xs_hbm, xs), (pick_hbm, pick),
            (spread_hbm, spread), (xf_hbm, xf), (xt_hbm, xt), (xi_hbm, xi), (yi_hbm, yi),
        ]
    ):
        copy = pltpu.make_async_copy(source, target, load_sem.at[index])
        copy.start()
        loads.append(copy)

    @pl.loop(0, FFT)
    def _(step):
        pl.semaphore_signal(barrier, inc=1, device_id=(fft_peer(step), other), device_id_type=MESH)

    @pl.loop(0, PLANES - 1)
    def _(step):
        pl.semaphore_signal(barrier, inc=1, device_id=(me, plane_peer(step)), device_id_type=MESH)

    def all_to_all(source, target, chunk, kind):
        @pl.loop(0, FFT)
        def _(step):
            peer = fft_peer(step)
            pltpu.make_async_remote_copy(
                src_ref=source.at[chunk, peer],
                dst_ref=target.at[chunk, me],
                send_sem=send_sem.at[kind, chunk],
                recv_sem=recv_sem.at[kind, chunk],
                device_id=(peer, other),
                device_id_type=MESH,
            ).start()

    def to_planes(source, target, chunk, kind):
        @pl.loop(0, PLANES - 1)
        def _(step):
            peer = plane_peer(step)
            pltpu.make_async_remote_copy(
                src_ref=source(peer),
                dst_ref=target,
                send_sem=send_sem.at[kind, chunk],
                recv_sem=recv_sem.at[kind, chunk],
                device_id=(me, peer),
                device_id_type=MESH,
            ).start()

    def wait_for(ref, sem):
        pltpu.make_async_copy(ref, ref, sem).wait()

    for copy in loads[:3]:
        copy.wait()
    operands = y_operands(field[:, 0, :], yt[0], yt[1])
    for index, operand in enumerate(operands):
        operand = split(operand)
        done = product((yf[0, :128], yf[1, :128]), operand, ((1,), (1,)))
        if index == 0:
            extra = product((yf[0, 128:], yf[1, 128:]), operand, ((1,), (1,)))[0:1, :]
            row = lax.broadcasted_iota(jnp.int32, (128, LANES), 0)
            lane = lax.broadcasted_iota(jnp.int32, (128, LANES), 1)
            done = jnp.where((row == 4) & (lane < HALF), extra, done)
        first = 16 * (index % 2)
        sent[index // 2, first : first + 16] = done.reshape(16, 8, LANES)
        if index == 1:
            pl.semaphore_wait(barrier, FFT + PLANES - 1)
        if index % 2 == 1:
            all_to_all(sent, received, index // 2, SEND)

    for copy in loads[3:]:
        copy.wait()
    row = lax.broadcasted_iota(jnp.int32, (8, LANES), 0) % 4
    lane = lax.broadcasted_iota(jnp.int32, (8, LANES), 1)
    x_here, x_other = x_factors(xs[...], pick[...], spread[...])
    for chunk in range(CHUNKS):
        here, opposite = jnp.zeros((8, LANES), F32), jnp.zeros((8, LANES), F32)
        group = 2 * chunk + me // 16
        for half in range(2):
            for step in range(4):
                line = 4 * lax.rem(me, 16) + step
                ky = jnp.where(group == 0, 8 * half + 16 * line, group + 16 * (line + 64 * half))
                place = (row == step) & (lane // HALF == half)
                here = jnp.where(place, y_shape[ky], here)
                opposite = jnp.where(place, y_shape[lax.rem(N - ky, N)], opposite)
        bound[0, chunk] = here[None] * x_here
        bound[1, chunk] = opposite[None] * x_other

    @pl.when(special)
    def _():
        here = jnp.where(lane < HALF, y_shape[0], y_shape[N // 2])
        bound[0, SPECIAL] = here[None] * x_here
        bound[1, SPECIAL] = here[None] * x_other

    def along_x(blocks, chunk):
        done = x_forward(blocks, (xf[0], xf[1]), xt)
        spec[chunk] = done
        real, imag = done[:, :, :LANES], done[:, :, LANES:]
        power[chunk] = real * real + imag * imag
        powers[chunk, plane] = power[chunk, plane]
        to_planes(lambda peer: power.at[chunk, peer], powers.at[chunk, plane], chunk, POWER)

    def forward(chunk):
        wait_for(received.at[chunk], recv_sem.at[SEND, chunk])
        along_x(received[chunk], chunk)

    def average(chunk):
        wait_for(powers.at[chunk, pl.ds(0, PLANES - 1)], recv_sem.at[POWER, chunk])
        total = powers[chunk, 0]
        for index in range(1, PLANES):
            total = total + powers[chunk, index]
        root[chunk, plane] = jnp.sqrt(total * (1.0 / PLANES))
        to_planes(lambda peer: root.at[chunk, plane], root.at[chunk, plane], chunk, MEAN)

    def clipped(chunk):
        wait_for(root.at[chunk, pl.ds(0, PLANES - 1)], recv_sem.at[MEAN, chunk])
        here, opposite = bound[0, chunk] * root[chunk], bound[1, chunk] * root[chunk]
        real, imag = spec[chunk, :, :, :LANES], spec[chunk, :, :, LANES:]
        return [
            0.5 * (jnp.clip(value, -here, here) + jnp.clip(value, -opposite, opposite)) for value in (real, imag)
        ]

    def backward(chunk):
        real, imag = clipped(chunk)
        sym[:, :, :LANES] = real
        sym[:, :, LANES:] = imag
        if chunk == 0:

            @pl.when(special)
            def _():
                real, imag = clipped(SPECIAL)
                place = (row == 0)[None] & (lane < HALF)[None]
                sym[:, :, :LANES] = jnp.where(place, real - pltpu.roll(imag, HALF, 2), sym[:, :, :LANES])
                sym[:, :, LANES:] = jnp.where(place, imag + pltpu.roll(real, HALF, 2), sym[:, :, LANES:])

        back[chunk] = x_inverse(sym[...], (xi[0], xi[1]), xt)
        all_to_all(back, returned, chunk, BACK)

    def along_y(chunk):
        wait_for(returned.at[chunk], recv_sem.at[BACK, chunk])
        for index in (2 * chunk, 2 * chunk + 1):
            first = 16 * (index % 2)
            rows = returned[chunk, first : first + 16].reshape(LANES, LANES)
            width = 2 * LANES if index else 3 * LANES
            total = product(split(rows), (yi[0, :, :width], yi[1, :, :width]), ((0,), (0,)))
            lines[index, 0], lines[index, 1] = y_line(total, index, yt[0], yt[1])

    forward(0)

    @pl.when(special)
    def _():
        blocks = received[0]
        turned = pltpu.roll(pltpu.roll(blocks, HALF, 2), 4, 1)
        blocks = jnp.where((lane < HALF)[None], blocks, turned)
        along_x(jnp.where(upper(blocks.shape), blocks, 0.0), SPECIAL)

    forward(1)
    average(0)

    @pl.when(special)
    def _():
        average(SPECIAL)

    forward(2)
    average(1)
    backward(0)
    forward(3)
    average(2)
    backward(1)
    average(3)
    backward(2)
    backward(3)

    for chunk in range(CHUNKS):
        along_y(chunk)
    for index, value in enumerate(y_result([(lines[index, 0], lines[index, 1]) for index in range(8)])):
        out[:, 0, LANES * index : LANES * (index + 1)] = value
    store = pltpu.make_async_copy(out, out_hbm, load_sem.at[0])
    store.start()

    for chunk in range(CHUNKS):
        for kind in (SEND, BACK):
            wait_for(received.at[chunk], send_sem.at[kind, chunk])
        for kind in (POWER, MEAN):
            wait_for(powers.at[chunk, pl.ds(0, PLANES - 1)], send_sem.at[kind, chunk])

    @pl.when(special)
    def _():
        for kind in (POWER, MEAN):
            wait_for(powers.at[SPECIAL, pl.ds(0, PLANES - 1)], send_sem.at[kind, SPECIAL])

    store.wait()


def correct(error_field, x_shape, y_shape):
    shape = error_field.shape
    operands = [
        error_field, y_forward_table(), y_inverse_table(), x_table(-1), x_table(1), y_twist(), x_twist(), *x_choices(),
        x_shape.reshape(16, LANES), y_shape,
    ]
    operands = [jnp.asarray(operand) for operand in operands]
    inside = [pltpu.VMEM(operand.shape, operand.dtype) for operand in operands]
    inside[-1] = pltpu.SMEM(y_shape.shape, F32)
    outside = pl.BlockSpec(memory_space=pltpu.HBM)
    return pl.pallas_call(
        kernel,
        out_shape=jax.ShapeDtypeStruct(shape, F32),
        in_specs=[outside] * len(operands),
        out_specs=outside,
        scratch_shapes=inside
        + [
            pltpu.VMEM(shape, F32),
            pltpu.VMEM((CHUNKS, FFT, 8, LANES), F32),
            pltpu.VMEM((CHUNKS, FFT, 8, LANES), F32),
            pltpu.VMEM((CHUNKS + 1, 16, 8, 2 * LANES), F32),
            pltpu.VMEM((CHUNKS + 1, PLANES, 8, LANES), F32),
            pltpu.VMEM((CHUNKS + 1, PLANES, 8, LANES), F32),
            pltpu.VMEM((CHUNKS + 1, PLANES, 8, LANES), F32),
            pltpu.VMEM((2, CHUNKS + 1, 16, 8, LANES), F32),
            pltpu.VMEM((CHUNKS, FFT, 8, LANES), F32),
            pltpu.VMEM((CHUNKS, FFT, 8, LANES), F32),
            pltpu.VMEM((16, 8, 2 * LANES), F32),
            pltpu.VMEM((8, 2, OWN, LANES), F32),
            pltpu.SemaphoreType.DMA((len(operands),)),
            pltpu.SemaphoreType.DMA((4, CHUNKS + 1)),
            pltpu.SemaphoreType.DMA((4, CHUNKS + 1)),
        ],
        compiler_params=pltpu.CompilerParams(
            collective_id=0, has_side_effects=True, vmem_limit_bytes=63 * 1024 * 1024
        ),
    )(*operands)


def solution(mesh):
    placed = (P("fft", "plane", None), P(), P())
    return jax.shard_map(
        correct, mesh=mesh, in_specs=placed, out_specs=P("fft", "plane", None), check_vma=False
    )
```

time: 71.3 us -> 56.2 us (0.79)
  Pallas kernels: 61.6 us -> 54.2 us
  local copies, waits for them, and re-layouts: 8.56 us -> 1.87 us
  other arithmetic: 0.73 us -> 0 us
    pallas_call x1, Pallas kernels: 61.6 us -> 54.2 us  [correct(): pl.pallas_call(kernel, out_shape=jax.ShapeDtypeStruct(shape, F32), in_spe...]
    unnamed x19 -> x1, local copies, waits for them, and re-layouts: 5.48 us -> 1.87 us
    slice x2 -> x0, local copies, waits for them, and re-layouts: 2.02 us -> none  [correct(): jnp.roll(x_shape[::-1], 1)]
    another operation x2 -> x0, local copies, waits for them, and re-layouts: 0.84 us -> none  [correct(): jnp.stack([x_shape, jnp.roll(x_shape[::-1], 1)]).reshape(2, HALF, FFT)]
    concatenate x1 -> x0, other arithmetic: 0.72 us -> none  [correct(): jnp.roll(x_shape[::-1], 1)]
where the time goes in v1:
time: 56.2 us; the launch traced here: 56 us
  Pallas kernels  54.2 us (96%)
  local copies, waits for them, and re-layouts  1.87 us (3%)
    pallas_call x1, Pallas kernels, correct(): pl.pallas_call(kernel, out_shape=jax.ShapeDtypeStruct(shape, F32), in_spe...  54.2 us
    unnamed x1, local copies, waits for them, and re-layouts  1.87 us

profile of v1, /device:TPU:1, one launch (start us, length us, event | category | flops | bytes accessed | tf_op | source)
XLA Modules:
  0.0 56.0 jit_solution(1633060569857730370)
XLA Ops:
  0.0 54.2 %shard_map.109 = f32[64,1,2048]{2,1,0:T(1,128)} custom-call(f32[64,1,2048]{2,1,0:T(1,128)} %field_hbm.1, bf16[2,144,256]{2,1,0:T(8,128)(2,1)} %constant.16.clone.yf_hbm, bf16[2,128,384]{2,1,0:T(8,128)(2,1)} %constant.17.clone.yi_hbm, bf16[2,256,256]{2,1,0:T(8,128)(2,1)} %constant.18.clone.xf_hbm, bf16[2,256,256]{2,1,0:T(8,128)(2,1)} %constant.19.clone.xi_hbm, ...), custom_call_target="tpu_custom_call" | custom-call | tf_op jit(solution)/shard_map/pallas_call | solution.py:503
  54.2 1.9 %copy.13 = f32[64,1,2048]{2,1,0:T(1,128)} copy(f32[64,1,2048]{2,1,0:T(1,128)} %shard_map.109) | data formatting | bytes 1048576

commit v2 on v1

--- a/solution.py
+++ b/solution.py
@@ -194,7 +194,7 @@
 
 
 def y_operands(field, twist_cos, twist_sin):
-    parts = real_dft([field[:, LANES * index : LANES * (index + 1)] for index in range(16)])
+    parts = real_dft(field)
     sign = 1.0 - 2.0 * (lax.broadcasted_iota(jnp.int32, (OWN, LANES), 1) % 2).astype(F32)
 
     def twisted(index):
@@ -283,8 +283,8 @@
 
 def kernel(
     field_hbm, yf_hbm, yi_hbm, xf_hbm, xi_hbm, yt_hbm, xt_hbm, pick_hbm, spread_hbm, xs_hbm, ys_hbm,
-    out_hbm,
-    field, yf, yi, xf, xi, yt, xt, pick, spread, xs, y_shape, out,
+    out,
+    field, yf, yi, xf, xi, yt, xt, pick, spread, xs, y_shape,
     sent, received, spec, power, powers, root, bound, back, returned, sym, lines,
     load_sem, send_sem, recv_sem,
 ):
@@ -350,7 +350,7 @@
 
     for copy in loads[:3]:
         copy.wait()
-    operands = y_operands(field[:, 0, :], yt[0], yt[1])
+    operands = y_operands([field[:, index, :] for index in range(16)], yt[0], yt[1])
     for index, operand in enumerate(operands):
         operand = split(operand)
         done = product((yf[0, :128], yf[1, :128]), operand, ((1,), (1,)))
@@ -461,8 +461,8 @@
 
     forward(2)
     average(1)
+    forward(3)
     backward(0)
-    forward(3)
     average(2)
     backward(1)
     average(3)
@@ -472,9 +472,7 @@
     for chunk in range(CHUNKS):
         along_y(chunk)
     for index, value in enumerate(y_result([(lines[index, 0], lines[index, 1]) for index in range(8)])):
-        out[:, 0, LANES * index : LANES * (index + 1)] = value
-    store = pltpu.make_async_copy(out, out_hbm, load_sem.at[0])
-    store.start()
+        out[:, index, :] = value
 
     for chunk in range(CHUNKS):
         for kind in (SEND, BACK):
@@ -487,27 +485,24 @@
         for kind in (POWER, MEAN):
             wait_for(powers.at[SPECIAL, pl.ds(0, PLANES - 1)], send_sem.at[kind, SPECIAL])
 
-    store.wait()
-
 
 def correct(error_field, x_shape, y_shape):
-    shape = error_field.shape
+    shape = (OWN, 16, LANES)
     operands = [
-        error_field, y_forward_table(), y_inverse_table(), x_table(-1), x_table(1), y_twist(), x_twist(), *x_choices(),
+        error_field.reshape(shape), y_forward_table(), y_inverse_table(), x_table(-1), x_table(1), y_twist(), x_twist(), *x_choices(),
         x_shape.reshape(16, LANES), y_shape,
     ]
     operands = [jnp.asarray(operand) for operand in operands]
     inside = [pltpu.VMEM(operand.shape, operand.dtype) for operand in operands]
     inside[-1] = pltpu.SMEM(y_shape.shape, F32)
     outside = pl.BlockSpec(memory_space=pltpu.HBM)
-    return pl.pallas_call(
+    done = pl.pallas_call(
         kernel,
-        out_shape=jax.ShapeDtypeStruct(shape, F32),
+        out_shape=pltpu.VMEM(shape, F32),
         in_specs=[outside] * len(operands),
-        out_specs=outside,
+        out_specs=pl.BlockSpec(memory_space=pltpu.VMEM),
         scratch_shapes=inside
         + [
-            pltpu.VMEM(shape, F32),
             pltpu.VMEM((CHUNKS, FFT, 8, LANES), F32),
             pltpu.VMEM((CHUNKS, FFT, 8, LANES), F32),
             pltpu.VMEM((CHUNKS + 1, 16, 8, 2 * LANES), F32),
@@ -524,9 +519,10 @@
             pltpu.SemaphoreType.DMA((4, CHUNKS + 1)),
         ],
         compiler_params=pltpu.CompilerParams(
-            collective_id=0, has_side_effects=True, vmem_limit_bytes=63 * 1024 * 1024
+            collective_id=0, has_side_effects=True, vmem_limit_bytes=60 * 1024 * 1024
         ),
     )(*operands)
+    return done.reshape(error_field.shape)
 
 
 def solution(mesh):

time: 56.2 us -> 52.2 us (0.929)
  Pallas kernels: 54.2 us -> 51.3 us
  local copies, waits for them, and re-layouts: 1.87 us -> 0.8 us
    pallas_call x1, Pallas kernels: 54.2 us -> 51.3 us  [correct(): pl.pallas_call(kernel, out_shape=pltpu.VMEM(shape, F32), in_specs=[outsid...]
    unnamed x1, local copies, waits for them, and re-layouts: 1.87 us -> 0.8 us
where the time goes in v2:
time: 52.2 us; the launch traced here: 52.1 us
  Pallas kernels  51.3 us (98%)
  local copies, waits for them, and re-layouts  0.8 us (2%)
    pallas_call x1, Pallas kernels, correct(): pl.pallas_call(kernel, out_shape=pltpu.VMEM(shape, F32), in_specs=[outsid...  51.3 us

profile of v2, /device:TPU:1, one launch (start us, length us, event | category | flops | bytes accessed | tf_op | source)
XLA Modules:
  0.0 52.1 jit_solution(17441065895544609529)
XLA Ops:
  0.0 51.3 %shard_map.109 = f32[64,16,128]{2,1,0:T(8,128)S(1)} custom-call(f32[64,16,128]{2,1,0:T(8,128)} %bitcast.4, bf16[2,144,256]{2,1,0:T(8,128)(2,1)} %constant.16.clone.yf_hbm, bf16[2,128,384]{2,1,0:T(8,128)(2,1)} %constant.17.clone.yi_hbm, bf16[2,256,256]{2,1,0:T(8,128)(2,1)} %constant.18.clone.xf_hbm, bf16[2,256,256]{2,1,0:T(8,128)(2,1)} %constant.19.clone.xi_hbm, ...), custom_call_target="tpu_custom_call" | custom-call | tf_op jit(solution)/shard_map/pallas_call | solution.py:499
  51.3 0.8 %copy.14 = f32[64,1,2048]{2,1,0:T(1,128)} copy(f32[64,1,2048]{2,1,0:T(1,128)S(1)} %bitcast.3) | data formatting | bytes 1048576

commit v3 on v2

--- a/solution.py
+++ b/solution.py
@@ -295,7 +295,9 @@
     barrier = pltpu.get_barrier_semaphore()
 
     def fft_peer(step):
-        return lax.rem(me // 4 + far_first(lax.rem(step, 8)), 8) * 4 + lax.rem(lax.rem(me, 4) + 1 + step // 8, 4)
+        part = step // 8
+        place = 2 * lax.rem(lax.rem(me, 4) // 2 + 1 + part, 2) + part // 2
+        return lax.rem(me // 4 + far_first(lax.rem(step, 8)), 8) * 4 + place
 
     def plane_peer(step):
         return lax.rem(plane // 2 + far_first(step // 2), 8) * 2 + lax.rem(plane + 1 + step, 2)
@@ -307,9 +309,9 @@
             (spread_hbm, spread), (xf_hbm, xf), (xt_hbm, xt), (xi_hbm, xi), (yi_hbm, yi),
         ]
     ):
-        copy = pltpu.make_async_copy(source, target, load_sem.at[index])
+        loads.append(pltpu.make_async_copy(source, target, load_sem.at[index]))
+    for copy in loads[:3]:
         copy.start()
-        loads.append(copy)
 
     @pl.loop(0, FFT)
     def _(step):
@@ -318,6 +320,9 @@
     @pl.loop(0, PLANES - 1)
     def _(step):
         pl.semaphore_signal(barrier, inc=1, device_id=(me, plane_peer(step)), device_id_type=MESH)
+
+    for copy in loads[3:]:
+        copy.start()
 
     def all_to_all(source, target, chunk, kind):
         @pl.loop(0, FFT)

time: 52.2 us -> 51.7 us (level)
  no operation moved by 1% of the time
where the time goes in v3:
time: 51.7 us; the launch traced here: 51.6 us
  Pallas kernels  50.8 us (98%)
  local copies, waits for them, and re-layouts  0.8 us (2%)
    pallas_call x1, Pallas kernels, correct(): pl.pallas_call(kernel, out_shape=pltpu.VMEM(shape, F32), in_specs=[outsid...  50.8 us

profile of v3, /device:TPU:1, one launch (start us, length us, event | category | flops | bytes accessed | tf_op | source)
XLA Modules:
  0.0 51.6 jit_solution(11947319266746752851)
XLA Ops:
  0.0 50.8 %shard_map.109 = f32[64,16,128]{2,1,0:T(8,128)S(1)} custom-call(f32[64,16,128]{2,1,0:T(8,128)} %bitcast.4, bf16[2,144,256]{2,1,0:T(8,128)(2,1)} %constant.16.clone.yf_hbm, bf16[2,128,384]{2,1,0:T(8,128)(2,1)} %constant.17.clone.yi_hbm, bf16[2,256,256]{2,1,0:T(8,128)(2,1)} %constant.18.clone.xf_hbm, bf16[2,256,256]{2,1,0:T(8,128)(2,1)} %constant.19.clone.xi_hbm, ...), custom_call_target="tpu_custom_call" | custom-call | tf_op jit(solution)/shard_map/pallas_call | solution.py:504
  50.8 0.8 %copy.14 = f32[64,1,2048]{2,1,0:T(1,128)} copy(f32[64,1,2048]{2,1,0:T(1,128)S(1)} %bitcast.3) | data formatting | bytes 1048576

commit v4 on v3

--- a/solution.py
+++ b/solution.py
@@ -313,13 +313,20 @@
     for copy in loads[:3]:
         copy.start()
 
-    @pl.loop(0, FFT)
-    def _(step):
-        pl.semaphore_signal(barrier, inc=1, device_id=(fft_peer(step), other), device_id_type=MESH)
-
-    @pl.loop(0, PLANES - 1)
-    def _(step):
-        pl.semaphore_signal(barrier, inc=1, device_id=(me, plane_peer(step)), device_id_type=MESH)
+    line, place = me // 4, lax.rem(me, 4)
+    ring, side = plane // 2, lax.rem(plane, 2)
+    partners = [
+        (min(along, 8 - along) + 1, lax.rem(line + along, 8) * 4 + lax.rem(place + turn_by, 4), other)
+        for along in range(8)
+        for turn_by in range(4)
+    ] + [
+        (min(along, 8 - along) + across, me, lax.rem(ring + along, 8) * 2 + lax.rem(side + across, 2))
+        for along in range(8)
+        for across in range(2)
+        if along + across
+    ]
+    for _, fft_index, plane_index in sorted(partners, key=lambda partner: -partner[0]):
+        pl.semaphore_signal(barrier, inc=1, device_id=(fft_index, plane_index), device_id_type=MESH)
 
     for copy in loads[3:]:
         copy.start()
@@ -465,12 +472,12 @@
         average(SPECIAL)
 
     forward(2)
+    forward(3)
     average(1)
-    forward(3)
+    average(2)
     backward(0)
-    average(2)
+    average(3)
     backward(1)
-    average(3)
     backward(2)
     backward(3)
 

time: 51.7 us -> 52.6 us (1.017)
  Pallas kernels: 50.8 us -> 51.7 us
    pallas_call x1, Pallas kernels: 50.8 us -> 51.7 us  [correct(): pl.pallas_call(kernel, out_shape=pltpu.VMEM(shape, F32), in_specs=[outsid...]
where the time goes in v4:
time: 52.6 us; the launch traced here: 52.5 us
  Pallas kernels  51.7 us (98%)
  local copies, waits for them, and re-layouts  0.8 us (2%)
    pallas_call x1, Pallas kernels, correct(): pl.pallas_call(kernel, out_shape=pltpu.VMEM(shape, F32), in_specs=[outsid...  51.7 us

profile of v4, /device:TPU:1, one launch (start us, length us, event | category | flops | bytes accessed | tf_op | source)
XLA Modules:
  0.0 52.5 jit_solution(14436027979597044968)
XLA Ops:
  0.0 51.7 %shard_map.109 = f32[64,16,128]{2,1,0:T(8,128)S(1)} custom-call(f32[64,16,128]{2,1,0:T(8,128)} %bitcast.4, bf16[2,144,256]{2,1,0:T(8,128)(2,1)} %constant.16.clone.yf_hbm, bf16[2,128,384]{2,1,0:T(8,128)(2,1)} %constant.17.clone.yi_hbm, bf16[2,256,256]{2,1,0:T(8,128)(2,1)} %constant.18.clone.xf_hbm, bf16[2,256,256]{2,1,0:T(8,128)(2,1)} %constant.19.clone.xi_hbm, ...), custom_call_target="tpu_custom_call" | custom-call | tf_op jit(solution)/shard_map/pallas_call | solution.py:511
  51.7 0.8 %copy.14 = f32[64,1,2048]{2,1,0:T(1,128)} copy(f32[64,1,2048]{2,1,0:T(1,128)S(1)} %bitcast.3) | data formatting | bytes 1048576

commit v5 on v4

--- a/solution.py
+++ b/solution.py
@@ -472,12 +472,12 @@
         average(SPECIAL)
 
     forward(2)
+    average(1)
     forward(3)
-    average(1)
+    backward(0)
     average(2)
-    backward(0)
+    backward(1)
     average(3)
-    backward(1)
     backward(2)
     backward(3)
 

time: 52.6 us -> 51 us (0.970)
  Pallas kernels: 51.7 us -> 50.1 us
    pallas_call x1, Pallas kernels: 51.7 us -> 50.1 us  [correct(): pl.pallas_call(kernel, out_shape=pltpu.VMEM(shape, F32), in_specs=[outsid...]
where the time goes in v5:
time: 51 us; the launch traced here: 50.9 us
  Pallas kernels  50.1 us (98%)
  local copies, waits for them, and re-layouts  0.8 us (2%)
    pallas_call x1, Pallas kernels, correct(): pl.pallas_call(kernel, out_shape=pltpu.VMEM(shape, F32), in_specs=[outsid...  50.1 us

profile of v5, /device:TPU:1, one launch (start us, length us, event | category | flops | bytes accessed | tf_op | source)
XLA Modules:
  0.0 50.9 jit_solution(4608411019130341791)
XLA Ops:
  0.0 50.1 %shard_map.109 = f32[64,16,128]{2,1,0:T(8,128)S(1)} custom-call(f32[64,16,128]{2,1,0:T(8,128)} %bitcast.4, bf16[2,144,256]{2,1,0:T(8,128)(2,1)} %constant.16.clone.yf_hbm, bf16[2,128,384]{2,1,0:T(8,128)(2,1)} %constant.17.clone.yi_hbm, bf16[2,256,256]{2,1,0:T(8,128)(2,1)} %constant.18.clone.xf_hbm, bf16[2,256,256]{2,1,0:T(8,128)(2,1)} %constant.19.clone.xi_hbm, ...), custom_call_target="tpu_custom_call" | custom-call | tf_op jit(solution)/shard_map/pallas_call | solution.py:511
  50.1 0.8 %copy.14 = f32[64,1,2048]{2,1,0:T(1,128)} copy(f32[64,1,2048]{2,1,0:T(1,128)S(1)} %bitcast.3) | data formatting | bytes 1048576
